TPU v7x, 256 devices: a whole 4x4x8 slice. The times are simulated.
256 devices in a mesh: ctx: 8 (over z_hi, core), ex: 32 (over y, z_lo, x).
Axes of the slice: x: 4, y: 4, z: 8 (z_hi: 4, z_lo: 2; z = z_hi * 2 + z_lo), core: 2. Of those that a mesh axis runs over, the one named last changes fastest.
Arguments:
- acts: bfloat16 [32, 1024, 8192], P('ex', 'ctx'), may hold values from -6 to 6
- out_grads: bfloat16 [32, 1024, 8192], P('ex', 'ctx'), may hold values from -6 to 6
- projections: bfloat16 [2, 8192, 256], P(None, 'ex', 'ctx'), may hold values from -0.0625 to 0.0625
- segments: int32 [32, 1024], P('ex', 'ctx'), may hold values from 0 to 3, never falling along the last dimension, each value on 1 to 512 neighbouring positions
- valid: int32 [32, 1024], P('ex', 'ctx'), may hold values 0 or 1
- stored: bfloat16 [98304, 8192], P('ex', 'ctx'), may hold values from -60 to 60, as said below
Outputs:
- scores: float32 [128, 98304], P('ctx', 'ex')
Inputs may be any that keep to these rules, and one draw needn't show every extreme that they name: `stored`: finite real values.
All inputs are finite; a program needn't handle non-finite values. No bound on the sum of `valid` on one device may be relied on, other than what follows from the above.
Results may differ from a plain program's by a relative error of at most 0.005.
Values may be sent and summed in bfloat16 or wider, within the bound.
A program may use at most 128 MiB of HBM per device.

v0:
```python
import math

import jax
import jax.numpy as jnp
from jax import lax
from jax.sharding import PartitionSpec as P

RANK = 32
MODULES = 8
DOCS = 4
STEPS = 4


damping = 0.1
spread = 1.5
epsilon = 1e-06


def shards(acts, out_grads, projections, segments, valid, stored):
    n_ex = lax.axis_size("ex")
    n_ctx = lax.axis_size("ctx")
    columns = lax.all_gather(projections, "ctx", axis=2, tiled=True)
    x_rows = acts[0]
    g_rows = out_grads[0]
    tok_count = x_rows.shape[0]
    col_count = columns.shape[2]
    weight_piece = lax.all_gather(columns, "ex", axis=1, tiled=True)
    x_term = jnp.dot(x_rows, weight_piece[0], preferred_element_type=jnp.float32)
    g_term = jnp.dot(g_rows, weight_piece[1], preferred_element_type=jnp.float32)
    projected = jnp.stack([x_term, g_term]).astype(jnp.bfloat16)
    modules_all = col_count // RANK
    doc_ids = jnp.arange(DOCS, dtype=jnp.int32)
    onehot = ((segments[0][None, :] == doc_ids[:, None]) & (valid[0][None, :] == 1)).astype(
        jnp.bfloat16
    )
    weighted = (onehot[:, :, None] * projected[1][None, :, :]).reshape(
        DOCS, tok_count, modules_all, RANK
    )
    partial_grads = jnp.einsum(
        "qtmi,tmj->qmij",
        weighted,
        projected[0].reshape(tok_count, modules_all, RANK),
        preferred_element_type=jnp.float32,
    ).reshape(DOCS, modules_all * RANK * RANK)
    queries = lax.psum_scatter(partial_grads, "ctx", scatter_dimension=1, tiled=True)
    feat_count = RANK * RANK
    mod_dev = queries.shape[1] // feat_count
    queries = queries.reshape(DOCS, mod_dev, feat_count)
    store_rows = stored.reshape(stored.shape[0], mod_dev, feat_count)
    local_gram = jnp.einsum(
        "smf,smg->mfg", store_rows, store_rows, preferred_element_type=jnp.float32
    )
    total_rows = stored.shape[0] * n_ex
    curvature = lax.psum(local_gram, "ex") / total_rows
    mean_diag = jnp.trace(curvature, axis1=1, axis2=2) / feat_count
    step_size = (1.0 / (spread * (mean_diag + epsilon)))[None, :, None]
    iterate = step_size * queries
    for iteration in range(STEPS):
        applied = (
            jnp.einsum("mfg,qmg->qmf", curvature, iterate, precision=lax.Precision.HIGHEST)
            + damping * mean_diag[None, :, None] * iterate
        )
        iterate = iterate + step_size * (queries - applied)
    precond = lax.all_gather(iterate.astype(jnp.bfloat16), "ex", axis=0, tiled=True)
    query_total = precond.shape[0]
    flat_queries = precond.reshape(query_total, mod_dev * feat_count)
    length_all = tok_count * n_ctx
    score_scale = 1.0 / math.sqrt(MODULES * feat_count * length_all / DOCS)
    query_part = lax.slice_in_dim(
        flat_queries, 0, query_total // n_ctx * lax.axis_size("ctx"), axis=0
    )
    summed_scores = lax.psum_scatter(
        lax.dot_general(
            query_part, stored, (((1,), (1,)), ((), ())), preferred_element_type=jnp.float32
        ),
        "ctx",
        scatter_dimension=0,
        tiled=True,
    )
    return summed_scores * score_scale


def solution(mesh):
    in_specs = (
        P("ex", "ctx", None),
        P("ex", "ctx", None),
        P(None, "ex", "ctx"),
        P("ex", "ctx"),
        P("ex", "ctx"),
        P("ex", "ctx"),
    )
    out_specs = P("ctx", "ex")
    return jax.shard_map(shards, mesh=mesh, in_specs=in_specs, out_specs=out_specs, check_vma=False)
```

profile of v0, /device:TPU:1, one launch (start us, length us, event | category | flops | bytes accessed | tf_op | source)
XLA Modules:
  0.0 737.7 jit_solution(11405952946229665443)
XLA Ops:
  6.5 0.0 copy-start
  6.5 0.0 all-gather.4.cloned.1.call-start
  6.5 21.1 %all_gather.9 = bf16[2,256,256]{1,2,0:T(8,128)(2,1)} all-gather(bf16[2,256,32]{1,2,0:T(8,128)(2,1)} %param.8), channel_id=1, replica_groups=mesh['ctx'=8,'ex'=32] {'ctx'}, dimensions={2}, use_global_device_ids=true | all-gather | bytes 294912 | tf_op jit(solution)/shard_map/all_gather | solution.py:22
  27.6 0.0 all-gather.4.cloned.1.call-update
  27.7 0.0 all-reduce.2.cloned.1.call-start
  27.7 12.2 %convolution_bitcast_fusion = f32[1,1024,1024]{2,1,0:T(8,128)} fusion(bf16[3072,1024]{1,0:T(8,128)(2,1)} %param.11), kind=kOutput, calls=%fused_computation.18 | convolution fusion | flops 6442450944 | bytes 10485760 | tf_op jit(solution)/shard_map/smf,smg->mfg/dot_general | solution.py:50
  39.9 0.0 copy-start.3
  39.9 0.0 copy-start.2
  39.9 0.0 all-reduce.2.cloned.1.call-update
  39.9 0.0 reduce-scatter.7.cloned.1.call-start
  40.0 0.6 copy-done.3
  40.6 0.0 copy-done.2
  40.6 139.0 %all-gather.4.cloned.1.call-done = bf16[2,8192,256]{1,2,0:T(8,128)(2,1)} async-done(((bf16[2,256,256]{1,2,0:T(8,128)(2,1)}), bf16[2,8192,256]{1,2,0:T(8,128)(2,1)}) %all-gather.4.cloned.1.call-update) | async-done | bytes 8388624 | tf_op jit(solution)/shard_map/all_gather | solution.py:27
  179.6 0.0 copy-done
  179.6 3.7 fusion.20
  183.3 0.1 copy.12
  183.5 4.4 fusion.23
  187.8 0.1 copy.13
  187.9 0.5 convolution_bitcast_fusion.1
  188.4 4.6 copy.18
  193.0 0.0 reduce-scatter.7.cloned.1.call-update
  193.0 0.2 reduce-scatter.5.cloned.1.call-start
  193.3 313.1 %all-reduce.2.cloned.1.call-done = f32[1,1024,1024]{2,1,0:T(8,128)} async-done(((f32[1,1024,1024]{2,1,0:T(8,128)}), f32[1,1024,1024]{2,1,0:T(8,128)}) %all-reduce.2.cloned.1.call-update) | async-done | bytes 4194320 | tf_op jit(solution)/shard_map/psum | solution.py:54
  506.4 2.9 select_reduce_fusion
  510.7 76.9 %reduce-scatter.7.cloned.1.call-done = f32[1024,4]{1,0:T(8,128)} async-done(((f32[8192,4]{1,0:T(8,128)}), f32[1024,4]{1,0:T(8,128)}) %reduce-scatter.7.cloned.1.call-update) | async-done | bytes 16400
  587.5 1.2 copy.17
  588.8 0.0 copy-start.1
  588.8 5.7 fusion.35
  594.5 0.0 copy-done.1
  594.5 3.4 fusion.47
  597.9 3.4 fusion.59
  601.3 3.4 fusion.77
  604.7 65.8 %all-gather.1 = bf16[32,4,1024]{2,1,0:T(4,128)(2,1)S(1)} all-gather(bf16[1,4,1024]{2,1,0:T(4,128)(2,1)S(1)} %fusion.77), channel_id=2, replica_groups=mesh['ctx'=8,'ex'=32] {'ex'}, dimensions={0}, use_global_device_ids=true | all-gather | bytes 270336 | tf_op jit(solution)/shard_map/all_gather | solution.py:64
  670.5 0.1 reshape.135
  670.6 6.1 fusion.91
  676.7 0.0 reduce-scatter.5.cloned.1.call-update
  676.8 52.7 %reduce-scatter.5.cloned.1.call-done = f32[16,3072]{1,0:T(8,128)} async-done(((f32[128,3072]{1,0:T(8,128)}), f32[16,3072]{1,0:T(8,128)}) %reduce-scatter.5.cloned.1.call-update) | async-done | bytes 196624 | tf_op jit(solution)/shard_map/reduce_scatter | solution.py:72
  729.5 1.6 broadcast_multiply_fusion
  (2 shorter events, 0.0 us)
Async XLA Ops:
  6.5 173.1 %copy-start = (bf16[1,128,8192]{2,1,0:T(8,128)(2,1)S(1)}, bf16[1,128,8192]{2,1,0:T(8,128)(2,1)}, u32[]{:S(2)}) copy-start(bf16[1,128,8192]{2,1,0:T(8,128)(2,1)} %param.6) | copy-start | bytes 6291460
  6.5 173.1 %all-gather.4.cloned.1.call-start = ((), (), s32[]{:S(2)}) async-start(), calls=%async_computation.3 | async-start | bytes 8650752 | tf_op jit(solution)/shard_map/all_gather | solution.py:27
  27.7 478.8 %all-reduce.2.cloned.1.call-start = ((), (), s32[]{:S(2)}) async-start(), calls=%async_computation.2 | async-start | bytes 8388608 | tf_op jit(solution)/shard_map/psum | solution.py:54
  39.9 0.7 copy-start.3
  39.9 0.7 copy-start.2
  39.9 547.6 %reduce-scatter.7.cloned.1.call-start = ((), (), s32[]{:S(2)}) async-start(), calls=%async_computation.5 | async-start | bytes 4718592
  193.0 536.5 %reduce-scatter.5.cloned.1.call-start = ((), (), s32[]{:S(2)}) async-start(), calls=%async_computation.4 | async-start | bytes 1769472 | tf_op jit(solution)/shard_map/reduce_scatter | solution.py:72
  588.8 5.7 copy-start.1
Sparse Core Ops, SparseCore 0:
  27.8 151.7 all-gather.3
  182.2 324.1 all-reduce.1
  509.0 78.5 reduce-scatter.6
  676.9 52.5 reduce-scatter.4
where the time goes:
time: 739 us; the launch traced here: 738 us
  waiting for transfers between devices  582 us (79%)
  blocking collectives  86.9 us (12%)
  matrix products  42.8 us (6%)
  between operations  14.6 us (2%)
    psum x1, waiting for transfers between devices, shards(): curvature = lax.psum(local_gram, 'ex') / total_rows  313 us
    all_gather x1, waiting for transfers between devices, shards(): weight_piece = lax.all_gather(columns, 'ex', axis=1, tiled=True)  139 us
    unnamed x5, waiting for transfers between devices  76.9 us
    all_gather x1, blocking collectives, shards(): lax.all_gather(iterate.astype(jnp.bfloat16), 'ex', axis=0, tiled=True)  65.8 us
    reduce_scatter x1, waiting for transfers between devices, shards(): lax.psum_scatter(lax.dot_general(query_part, stored, (((1,), (1,)), ((),...  52.7 us
    all_gather x1, blocking collectives, shards(): columns = lax.all_gather(projections, 'ctx', axis=2, tiled=True)  21.1 us
    dot_general x4, matrix products, shards(): jnp.einsum('mfg,qmg->qmf', curvature, iterate, precision=lax.Precision.HI...  15.9 us
  transfers between devices with their start and end apart: 4, of which 4 were waited for; matrix products, arithmetic and copies ran while one was open for 4% of the time, Pallas kernels for 0%

commit v1 on v0

v1 whole, which is shorter than its diff:
```python
import math

import jax
import jax.numpy as jnp
from jax import lax
from jax.experimental import pallas as pl
from jax.experimental.pallas import tpu as pltpu
from jax.sharding import PartitionSpec as P

RANK = 32
MODULES = 8
DOCS = 4
STEPS = 4
FEAT = 1024
STORE = 98304
LEN = 1024

damping = 0.1
spread = 1.5
epsilon = 1e-06

MESH = pl.DeviceIdType.MESH
F32 = jnp.float32
BF16 = jnp.bfloat16

N_EX = 32
CHUNKS = 4
BLK = 256
NBLK = FEAT // BLK
PAIRS = [(i, j) for i in range(NBLK) for j in range(i, NBLK)]
PIECE = len(PAIRS) * BLK // N_EX

NN = (((1,), (0,)), ((), ()))
NT = (((1,), (1,)), ((), ()))
TN = (((0,), (0,)), ((), ()))


def dot(a, b, dims):
    return lax.dot_general(a, b, dims, preferred_element_type=F32)


def kernel(
    pt, acts, grads, seg, val, stored, out,
    wa, wb, xa, ga, sv, wm, gsend, grecv, cb, tsend, trecv, qs, qg, part, sib, zsend, zrecv,
    loc_sem, sib_s, sib_r, z_s, z_r, ring_s, ring_r, g_s, g_r, c_s, c_r, t_s, t_r, q_s, q_r,
    o_s, o_r, zo_s, zo_r,
):
    ctx = lax.axis_index("ctx")
    ex = lax.axis_index("ex")
    zh, core = ctx // 2, ctx % 2
    y, zl, x = ex // 8, (ex // 4) % 2, ex % 4
    z = zh * 2 + zl

    def at(xx, yy, zz):
        return {"ctx": (zz // 2) * 2 + core, "ex": (yy * 2 + zz % 2) * 4 + xx}

    sibling = {"ctx": zh * 2 + 1 - core, "ex": ex}

    def remote(src, dst, s, r, device):
        return pltpu.make_async_remote_copy(
            src_ref=src, dst_ref=dst, send_sem=s, recv_sem=r, device_id=device, device_id_type=MESH
        )

    load_s = pltpu.make_async_copy(stored, sv, loc_sem.at[0])
    load_x = pltpu.make_async_copy(acts.at[0], xa.at[0], loc_sem.at[1])
    load_g = pltpu.make_async_copy(grads.at[0], ga.at[0], loc_sem.at[2])
    load_s.start()
    load_x.start()
    load_g.start()

    barrier = pltpu.get_barrier_semaphore()

    def greet(k, carry):
        pl.semaphore_signal(
            barrier, inc=1, device_id={"ctx": ctx, "ex": (ex + k) % N_EX}, device_id_type=MESH
        )
        return carry

    lax.fori_loop(1, N_EX, greet, 0)
    for dh in range(1, 4):
        for l in range(2):
            pl.semaphore_signal(
                barrier, inc=1, device_id=at(x, y, ((zh + dh) % 4) * 2 + l), device_id_type=MESH
            )
    pl.semaphore_signal(barrier, inc=1, device_id=sibling, device_id_type=MESH)
    for d in range(8):
        wm[0, d : d + 1, :] = jnp.where((seg[...] == d) & (val[...] == 1), 1.0, 0.0).astype(F32)
    wa[x, y, zl, zh] = pt[0]
    wb[y, x, zl, zh] = pt[1]
    pl.semaphore_wait(barrier, N_EX - 1 + 7)

    swaps = [
        remote(acts.at[0], xa.at[1], sib_s.at[0], sib_r.at[0], sibling),
        remote(grads.at[0], ga.at[1], sib_s.at[1], sib_r.at[1], sibling),
        remote(wm.at[0], wm.at[1], sib_s.at[2], sib_r.at[2], sibling),
    ]

    def along_z(d, a):
        slot = wa.at[x, y, zl, zh] if a == 0 else wb.at[y, x, zl, zh]
        return remote(pt.at[a], slot, z_s.at[a, d], z_r.at[a, d], at(x, y, (z + d) % 8))

    def z_arrival(d, a):
        zz = (z + 8 - d) % 8
        slot = wa.at[x, y, zz % 2, zz // 2] if a == 0 else wb.at[y, x, zz % 2, zz // 2]
        return remote(pt.at[a], slot, z_s.at[a, d], z_r.at[a, d], at(x, y, zz))

    for d in (1, 7, 2, 6, 3, 5, 4):
        for a in range(2):
            along_z(d, a).start()
    for copy in swaps:
        copy.start()

    xp_, xm, xo = (x + 1) % 4, (x + 3) % 4, (x + 2) % 4
    yp_, ym, yo = (y + 1) % 4, (y + 3) % 4, (y + 2) % 4

    def ring_pairs(block, half, where, me, plus, minus, opposite, first):
        def one(ref, k, device):
            return remote(ref, ref, ring_s.at[first + k], ring_r.at[first + k], device)

        own = [one(block(me), 0, where(plus)), one(block(me), 1, where(minus))]
        onward = [one(half(minus, 0), 2, where(plus)), one(half(plus, 1), 3, where(minus))]
        own_in = [one(block(minus), 0, where(minus)), one(block(plus), 1, where(plus))]
        onward_in = [one(half(opposite, 0), 2, where(minus)), one(half(opposite, 1), 3, where(plus))]
        return own, onward, own_in, onward_in

    ay = ring_pairs(
        lambda i: wa.at[x, i], lambda i, h: wa.at[x, i, h], lambda i: at(x, i, z), y, yp_, ym, yo, 0
    )
    bx = ring_pairs(
        lambda i: wb.at[y, i], lambda i, h: wb.at[y, i, h], lambda i: at(i, y, z), x, xp_, xm, xo, 4
    )
    ax = ring_pairs(
        lambda i: wa.at[i], lambda i, h: wa.at[i, 2 * h : 2 * h + 2], lambda i: at(i, y, z), x, xp_, xm, xo, 8
    )
    by = ring_pairs(
        lambda i: wb.at[i], lambda i, h: wb.at[i, 2 * h : 2 * h + 2], lambda i: at(x, i, z), y, yp_, ym, yo, 12
    )

    def gram(first, last):
        for n in range(first, last):
            i, j = PAIRS[n]
            gsend[n * BLK : (n + 1) * BLK, :] = dot(
                sv[:, i * BLK : (i + 1) * BLK], sv[:, j * BLK : (j + 1) * BLK], TN
            ).astype(BF16)

    def begin(two):
        for pair in zip(*two):
            for copy in pair:
                copy.start()

    def arrived(two):
        for pair in zip(*two):
            for copy in pair:
                copy.wait_recv()

    load_s.wait()
    gram(0, 2)
    for d in (1, 7, 2, 6, 3, 5, 4):
        for a in range(2):
            z_arrival(d, a).wait_recv()
    begin((ay[0], bx[0]))
    gram(2, 5)
    arrived((ay[2], bx[2]))
    begin((ay[1], bx[1]))
    gram(5, 7)
    arrived((ay[3], bx[3]))
    begin((ax[0], by[0]))
    gram(7, 10)

    def piece(ref, k):
        return ref.at[pl.ds(pl.multiple_of(k * PIECE, 16), PIECE), :]

    def gram_out(k):
        to = (ex + k) % N_EX
        return remote(piece(gsend, to), grecv.at[k], g_s.at[k], g_r.at[k], {"ctx": ctx, "ex": to})

    def sum_out(k):
        to = (ex + k) % N_EX
        return remote(piece(cb, ex), piece(cb, ex), c_s.at[k], c_r.at[k], {"ctx": ctx, "ex": to})

    def sum_in(k):
        of = (ex + N_EX - k) % N_EX
        return remote(piece(cb, of), piece(cb, of), c_s.at[k], c_r.at[k], {"ctx": ctx, "ex": of})

    def loop(body):
        def step(k, carry):
            body(k)
            return carry

        lax.fori_loop(1, N_EX, step, 0)

    loop(lambda k: gram_out(k).start())
    arrived((ax[2], by[2]))
    begin((ax[1], by[1]))
    def add_piece(k, total):
        gram_out(k).wait_recv()
        return total + grecv[k].astype(F32)

    own_piece = gsend[pl.ds(pl.multiple_of(ex * PIECE, 16), PIECE), :].astype(F32)
    total = lax.fori_loop(1, N_EX, add_piece, own_piece)
    cb[pl.ds(pl.multiple_of(ex * PIECE, 16), PIECE), :] = total.astype(BF16)
    loop(lambda k: sum_out(k).start())

    load_x.wait()
    load_g.wait()
    for copy in swaps:
        copy.wait_recv()
    arrived((ax[3], by[3]))
    rows = 2 * 128

    def project(n, carry):
        xt, gt = carry
        yy, xx = n // 4, n % 4
        for l in range(2):
            e = (yy * 2 + l) * 4 + xx
            cols = pl.ds(pl.multiple_of(e * 256, 256), 256)
            xt = xt + dot(xa[:, :, cols].reshape(rows, 256), wa[xx, yy, l].reshape(128, 256), NT)
            gt = gt + dot(wb[yy, xx, l].reshape(128, 256), ga[:, :, cols].reshape(rows, 256), NT)
        return xt, gt

    xt, gt = lax.fori_loop(0, 16, project, (jnp.zeros((rows, 128), F32), jnp.zeros((128, rows), F32)))
    xt, gt = xt.astype(BF16), gt.astype(BF16)
    weights = jnp.concatenate([wm[0], wm[1]], axis=1)
    lane = lax.broadcasted_iota(jnp.int32, (32, 128), 1) // 32
    outer = [
        dot((gt.astype(F32) * weights[d : d + 1, :]).astype(BF16), xt, NN) for d in range(DOCS)
    ]
    for h in range(4):
        packed = jnp.zeros((32, 128), F32)
        for d in range(DOCS):
            block = outer[d][h * 32 : (h + 1) * 32, :]
            shift = ((d - h) * 32) % 128
            if shift:
                block = pltpu.roll(block, shift, 1)
            packed = jnp.where(lane == d, block, packed)
        tsend[h] = packed

    def t_out(k):
        to = (zh + k) % 4
        return remote(tsend.at[to], trecv.at[k], t_s.at[k], t_r.at[k], at(x, y, to * 2 + zl))

    for k in (1, 3, 2):
        t_out(k).start()
    spread_lanes = (
        lax.broadcasted_iota(jnp.int32, (128, FEAT), 0) == lax.broadcasted_iota(jnp.int32, (128, FEAT), 1) % 32
    ).astype(F32).astype(BF16)
    keep = lax.broadcasted_iota(jnp.int32, (32, FEAT), 0) == lax.broadcasted_iota(jnp.int32, (32, FEAT), 1) // 32
    grad_sum = tsend[zh]
    for k in (1, 3, 2):
        t_out(k).wait_recv()
        grad_sum = grad_sum + trecv[k]
    high = grad_sum.astype(BF16).astype(F32)
    rest = grad_sum - high
    middle = rest.astype(BF16).astype(F32)
    low = rest - middle
    for d in range(DOCS):
        turned = [pltpu.roll(p, (128 - d * 32) % 128, 1) if d else p for p in (high, middle, low)]
        wide = dot(jnp.concatenate(turned, axis=0).astype(BF16), spread_lanes, NN)
        wide = wide[0:32] + wide[32:64] + wide[64:96]
        row = jnp.sum(jnp.where(keep, wide, 0.0), axis=0, keepdims=True)
        for k in range(8):
            qs[d * 8 + k : d * 8 + k + 1, :] = row[:, k * 128 : (k + 1) * 128]

    def queries_at(e):
        return qg.at[pl.ds(pl.multiple_of(e * 32, 32), 32), :]

    def q_out(k):
        return remote(qs, queries_at(ex), q_s.at[k], q_r.at[k], {"ctx": ctx, "ex": (ex + k) % N_EX})

    def q_in(k):
        of = (ex + N_EX - k) % N_EX
        return remote(qs, queries_at(of), q_s.at[k], q_r.at[k], {"ctx": ctx, "ex": of})

    loop(lambda k: q_out(k).start())
    qg[pl.ds(pl.multiple_of(ex * 32, 32), 32), :] = qs[...]
    loop(lambda k: sum_in(k).wait_recv())
    loop(lambda k: q_in(k).wait_recv())

    def curv(j, i):
        n = PAIRS.index((min(i, j), max(i, j)))
        return cb[n * BLK : (n + 1) * BLK, :], (NN if j <= i else NT)

    diagonal = lax.broadcasted_iota(jnp.int32, (BLK, BLK), 0) == lax.broadcasted_iota(jnp.int32, (BLK, BLK), 1)
    trace = jnp.zeros((1, 1), F32)
    for i in range(NBLK):
        kept = jnp.where(diagonal, curv(i, i)[0].astype(F32), 0.0)
        trace = trace + jnp.sum(jnp.sum(kept, axis=0, keepdims=True), axis=1, keepdims=True)
    mean_diag = trace / STORE / FEAT
    step_size = 1.0 / (spread * (mean_diag + epsilon))

    queries = [
        jnp.concatenate([qg[pl.ds(2 * i + h, 128, stride=8), :] for h in range(2)], axis=1) for i in range(NBLK)
    ]
    iterate = [step_size * q for q in queries]
    for _ in range(STEPS):
        split = []
        for v in iterate:
            top = v.astype(BF16)
            split.append(jnp.concatenate([top, (v - top.astype(F32)).astype(BF16)], axis=0))
        following = []
        for i in range(NBLK):
            both = jnp.zeros((256, BLK), F32)
            for j in range(NBLK):
                block, dims = curv(j, i)
                both = both + dot(split[j], block, dims)
            applied = (both[:128] + both[128:]) / STORE + damping * mean_diag * iterate[i]
            following.append(iterate[i] + step_size * (queries[i] - applied))
        iterate = following
    precond = jnp.concatenate([v.astype(BF16) for v in iterate], axis=1)

    width = 3072 // CHUNKS

    def o_out(n):
        return remote(part.at[n, 1 - core], sib.at[n], o_s.at[n], o_r.at[n], sibling)

    def zo_out(n, k):
        to = (zh + k) % 4
        return remote(zsend.at[n, to], zrecv.at[n, k], zo_s.at[n, k], zo_r.at[n, k], at(x, y, to * 2 + zl))

    def hand_on(n):
        o_out(n).wait_recv()
        for h in range(4):
            zsend[n, h] = (part[n, core, h] + sib[n, h]).astype(BF16)
        for k in (2, 1, 3):
            zo_out(n, k).start()

    for n in range(CHUNKS):
        scores = dot(precond, sv[n * width : (n + 1) * width, :], NT)
        for c in range(8):
            part[n, c % 2, c // 2] = scores[c * 16 : (c + 1) * 16, :]
        o_out(n).start()
        if n:
            hand_on(n - 1)
    hand_on(CHUNKS - 1)
    score_scale = 1.0 / math.sqrt(MODULES * FEAT * LEN / DOCS)
    for n in range(CHUNKS):
        own = part[n, core, zh] + sib[n, zh]
        for k in (1, 3, 2):
            zo_out(n, k).wait_recv()
            own = own + zrecv[n, k].astype(F32)
        out[:, n * width : (n + 1) * width] = own * score_scale

    for d in range(1, 8):
        for a in range(2):
            along_z(d, a).wait_send()
    for copy in swaps:
        copy.wait_send()
    for four in (ay, bx, ax, by):
        for copy in four[0] + four[1]:
            copy.wait_send()
    loop(lambda k: gram_out(k).wait_send())
    loop(lambda k: sum_out(k).wait_send())
    loop(lambda k: q_out(k).wait_send())
    for k in (1, 2, 3):
        t_out(k).wait_send()
        for n in range(CHUNKS):
            zo_out(n, k).wait_send()
    for n in range(CHUNKS):
        o_out(n).wait_send()


def shards(acts, out_grads, projections, segments, valid, stored):
    columns = jnp.transpose(projections, (0, 2, 1))
    vmem = pl.BlockSpec(memory_space=pltpu.VMEM)
    hbm = pl.BlockSpec(memory_space=pl.ANY)
    dma = pltpu.SemaphoreType.DMA
    width = 3072 // CHUNKS
    return pl.pallas_call(
        kernel,
        out_shape=jax.ShapeDtypeStruct((16, 3072), F32),
        in_specs=[vmem, hbm, hbm, vmem, vmem, hbm],
        out_specs=vmem,
        scratch_shapes=[
            pltpu.VMEM((4, 4, 2, 4, 32, 256), BF16),
            pltpu.VMEM((4, 4, 2, 4, 32, 256), BF16),
            pltpu.VMEM((2, 128, 8192), BF16),
            pltpu.VMEM((2, 128, 8192), BF16),
            pltpu.VMEM((3072, FEAT), BF16),
            pltpu.VMEM((2, 8, 128), F32),
            pltpu.VMEM((N_EX * PIECE, BLK), BF16),
            pltpu.VMEM((N_EX, PIECE, BLK), BF16),
            pltpu.VMEM((N_EX * PIECE, BLK), BF16),
            pltpu.VMEM((4, 32, 128), F32),
            pltpu.VMEM((4, 32, 128), F32),
            pltpu.VMEM((32, 128), F32),
            pltpu.VMEM((N_EX * 32, 128), F32),
            pltpu.VMEM((CHUNKS, 2, 4, 16, width), F32),
            pltpu.VMEM((CHUNKS, 4, 16, width), F32),
            pltpu.VMEM((CHUNKS, 4, 16, width), BF16),
            pltpu.VMEM((CHUNKS, 4, 16, width), BF16),
            dma((3,)),
            dma((3,)),
            dma((3,)),
            dma((2, 8)),
            dma((2, 8)),
            dma((16,)),
            dma((16,)),
            dma((N_EX,)),
            dma((N_EX,)),
            dma((N_EX,)),
            dma((N_EX,)),
            dma((4,)),
            dma((4,)),
            dma((N_EX,)),
            dma((N_EX,)),
            dma((CHUNKS,)),
            dma((CHUNKS,)),
            dma((CHUNKS, 4)),
            dma((CHUNKS, 4)),
        ],
        compiler_params=pltpu.CompilerParams(
            collective_id=0, has_side_effects=True, vmem_limit_bytes=50 * 1024 * 1024
        ),
        cost_estimate=pl.CostEstimate(flops=12_000_000_000, bytes_accessed=20_000_000, transcendentals=0),
    )(columns, acts, out_grads, segments, valid, stored)


def solution(mesh):
    in_specs = (
        P("ex", "ctx", None),
        P("ex", "ctx", None),
        P(None, "ex", "ctx"),
        P("ex", "ctx"),
        P("ex", "ctx"),
        P("ex", "ctx"),
    )
    out_specs = P("ctx", "ex")
    return jax.shard_map(shards, mesh=mesh, in_specs=in_specs, out_specs=out_specs, check_vma=False)
```

time: 739 us -> 117 us (0.16)
  waiting for transfers between devices: 582 us -> 0 us
  Pallas kernels: 0 us -> 113 us
  blocking collectives: 86.9 us -> 0 us
  matrix products: 42.8 us -> 0 us
  between operations: 14.6 us -> 0.01 us
    psum x1 -> x0, waiting for transfers between devices: 313 us -> none  [shards(): curvature = lax.psum(local_gram, 'ex') / total_rows]
    all_gather x1 -> x0, waiting for transfers between devices: 139 us -> none  [shards(): weight_piece = lax.all_gather(columns, 'ex', axis=1, tiled=True)]
    pallas_call x0 -> x1, Pallas kernels: none -> 113 us  [shards(): pl.pallas_call(kernel, out_shape=jax.ShapeDtypeStruct((16, 3072), F32), i...]
    all_gather x2 -> x0, blocking collectives: 86.9 us -> none  [the longest x1 65.8 us: shards(): lax.all_gather(iterate.astype(jnp.bfloat16), 'ex', axis=0, tiled=True)]
    unnamed x5 -> x0, waiting for transfers between devices: 76.9 us -> none
    reduce_scatter x1 -> x0, waiting for transfers between devices: 52.7 us -> none  [shards(): lax.psum_scatter(lax.dot_general(query_part, stored, (((1,), (1,)), ((),...]
    dot_general x9 -> x0, matrix products: 42.8 us -> none  [the longest x4 15.9 us: shards(): jnp.einsum('mfg,qmg->qmf', curvature, iterate, precision=lax.Precision.HI...]
  transfers between devices with their start and end apart: 4 -> 0, of which waited for: 4 -> 0; matrix products, arithmetic and copies ran while one was open for 4% -> 0% of each run, Pallas kernels for 0% -> 0%
where the time goes in v1:
time: 117 us
  Pallas kernels  113 us (97%)
  local copies, waits for them, and re-layouts  4.34 us (4%)
    pallas_call x1, Pallas kernels, shards(): pl.pallas_call(kernel, out_shape=jax.ShapeDtypeStruct((16, 3072), F32), i...  113 us
    unnamed x9, local copies, waits for them, and re-layouts  4.34 us

profile of v1, /device:TPU:1, one launch (start us, length us, event | category | flops | bytes accessed | tf_op | source)
XLA Modules:
  0.0 117.0 jit_solution(8452713972830821779)
XLA Ops:
  0.0 0.0 copy-start
  0.0 1.6 %copy-done = bf16[1,128,8192]{2,1,0:T(8,128)(2,1)S(1)} copy-done((bf16[1,128,8192]{2,1,0:T(8,128)(2,1)S(1)}, bf16[1,128,8192]{2,1,0:T(8,128)(2,1)}, u32[]{:S(2)}) %copy-start) | copy-done | bytes 2097176
  1.6 0.0 copy-start.1
  1.6 0.8 copy-done.1
  2.4 0.0 copy-start.2
  2.4 0.7 copy-done.2
  3.0 0.0 copy-start.3
  3.0 0.7 copy-done.3
  3.7 112.7 %shard_map.64 = f32[16,3072]{1,0:T(8,128)S(1)} custom-call(bf16[2,32,256]{2,1,0:T(8,128)(2,1)S(1)} %bitcast.1, bf16[1,128,8192]{2,1,0:T(8,128)(2,1)S(1)} %copy-done, bf16[1,128,8192]{2,1,0:T(8,128)(2,1)} %grads.1, s32[1,128]{1,0:T(1,128)S(1)} %copy-done.2, s32[1,128]{1,0:T(1,128)S(1)} %copy-done.3, bf16[3072,1024]{1,0:T(8,128)(2,1)} %stored.1), custom_call_target="tpu_custom_call" | custom-call | flops 12000000000 | bytes 20000000 | tf_op jit(solution)/shard_map/pallas_call | solution.py:368
  116.3 0.7 copy.8
Async XLA Ops:
  0.0 1.6 %copy-start = (bf16[1,128,8192]{2,1,0:T(8,128)(2,1)S(1)}, bf16[1,128,8192]{2,1,0:T(8,128)(2,1)}, u32[]{:S(2)}) copy-start(bf16[1,128,8192]{2,1,0:T(8,128)(2,1)} %acts.1) | copy-start | bytes 6291460
  1.6 0.8 copy-start.1
  2.4 0.7 copy-start.2
  3.0 0.7 copy-start.3

commit v2 on v1

--- a/solution.py
+++ b/solution.py
@@ -28,7 +28,9 @@
 BLK = 256
 NBLK = FEAT // BLK
 PAIRS = [(i, j) for i in range(NBLK) for j in range(i, NBLK)]
-PIECE = len(PAIRS) * BLK // N_EX
+HALF = len(PAIRS) * BLK // 2
+LONG = HALF // 4
+SHORT = LONG // 4
 
 NN = (((1,), (0,)), ((), ()))
 NT = (((1,), (1,)), ((), ()))
@@ -41,8 +43,8 @@
 
 def kernel(
     pt, acts, grads, seg, val, stored, out,
-    wa, wb, xa, ga, sv, wm, gsend, grecv, cb, tsend, trecv, qs, qg, part, sib, zsend, zrecv,
-    loc_sem, sib_s, sib_r, z_s, z_r, ring_s, ring_r, g_s, g_r, c_s, c_r, t_s, t_r, q_s, q_r,
+    wa, wb, xa, ga, sv, sg, vl, wm, gsend, r1, s1, r2, s2, r3, cb, tsend, trecv, qs, qg, part, sib, zsend, zrecv,
+    loc_sem, sib_s, sib_r, z_s, z_r, ring_s, ring_r, rs_s, rs_r, zl_s, zl_r, ag_s, ag_r, t_s, t_r, q_s, q_r,
     o_s, o_r, zo_s, zo_r,
 ):
     ctx = lax.axis_index("ctx")
@@ -64,9 +66,12 @@
     load_s = pltpu.make_async_copy(stored, sv, loc_sem.at[0])
     load_x = pltpu.make_async_copy(acts.at[0], xa.at[0], loc_sem.at[1])
     load_g = pltpu.make_async_copy(grads.at[0], ga.at[0], loc_sem.at[2])
-    load_s.start()
-    load_x.start()
-    load_g.start()
+    load_a = pltpu.make_async_copy(pt.at[0], wa.at[x, y, zl, zh], loc_sem.at[3])
+    load_b = pltpu.make_async_copy(pt.at[1], wb.at[y, x, zl, zh], loc_sem.at[4])
+    load_seg = pltpu.make_async_copy(seg, sg, loc_sem.at[5])
+    load_val = pltpu.make_async_copy(val, vl, loc_sem.at[6])
+    for copy in (load_seg, load_val, load_a, load_b, load_s, load_x, load_g):
+        copy.start()
 
     barrier = pltpu.get_barrier_semaphore()
 
@@ -83,10 +88,10 @@
                 barrier, inc=1, device_id=at(x, y, ((zh + dh) % 4) * 2 + l), device_id_type=MESH
             )
     pl.semaphore_signal(barrier, inc=1, device_id=sibling, device_id_type=MESH)
+    load_seg.wait()
+    load_val.wait()
     for d in range(8):
-        wm[0, d : d + 1, :] = jnp.where((seg[...] == d) & (val[...] == 1), 1.0, 0.0).astype(F32)
-    wa[x, y, zl, zh] = pt[0]
-    wb[y, x, zl, zh] = pt[1]
+        wm[0, d : d + 1, :] = jnp.where((sg[...] == d) & (vl[...] == 1), 1.0, 0.0).astype(F32)
     pl.semaphore_wait(barrier, N_EX - 1 + 7)
 
     swaps = [
@@ -104,8 +109,9 @@
         slot = wa.at[x, y, zz % 2, zz // 2] if a == 0 else wb.at[y, x, zz % 2, zz // 2]
         return remote(pt.at[a], slot, z_s.at[a, d], z_r.at[a, d], at(x, y, zz))
 
-    for d in (1, 7, 2, 6, 3, 5, 4):
-        for a in range(2):
+    far = (4, 3, 5, 2, 6, 1, 7)
+    for a in range(2):
+        for d in far:
             along_z(d, a).start()
     for copy in swaps:
         copy.start()
@@ -153,72 +159,110 @@
             for copy in pair:
                 copy.wait_recv()
 
+    def along(half, stage, to):
+        return at(to, y, z) if half == stage else at(x, to, z)
+
+    def place(half, stage):
+        return x if half == stage else y
+
+    def rows_of(ref, first, count):
+        return ref.at[pl.ds(pl.multiple_of(first, 16), count), :]
+
+    def gram_out(half, k):
+        to = (place(half, 0) + k) % 4
+        source = rows_of(gsend, half * HALF + to * LONG, LONG)
+        return remote(source, r1.at[half, k], rs_s.at[half, 0, k], rs_r.at[half, 0, k], along(half, 0, to))
+
+    def part_out(half, k):
+        to = (place(half, 1) + k) % 4
+        source = rows_of(s1.at[half], to * SHORT, SHORT)
+        return remote(source, r2.at[half, k], rs_s.at[half, 1, k], rs_r.at[half, 1, k], along(half, 1, to))
+
+    def pair_out(half):
+        return remote(s2.at[half], r3.at[half], zl_s.at[half], zl_r.at[half], at(x, y, zh * 2 + 1 - zl))
+
+    def short_block(half, j):
+        return rows_of(cb, half * HALF + place(half, 0) * LONG + j * SHORT, SHORT)
+
+    def long_block(half, j):
+        return rows_of(cb, half * HALF + j * LONG, LONG)
+
+    def spread_out(half, stage, k, arriving=False):
+        me = place(half, stage)
+        block = (long_block, short_block)[stage](half, (me + 4 - k) % 4 if arriving else me)
+        to = (me + k) % 4
+        return remote(block, block, ag_s.at[half, stage, k], ag_r.at[half, stage, k], along(half, stage, to))
+
+    around = (2, 1, 3)
     load_s.wait()
-    gram(0, 2)
-    for d in (1, 7, 2, 6, 3, 5, 4):
-        for a in range(2):
+    for half in range(2):
+        gram(5 * half, 5 * half + 5)
+        for k in around:
+            gram_out(half, k).start()
+    load_a.wait()
+    load_b.wait()
+    for a in range(2):
+        for d in far:
             z_arrival(d, a).wait_recv()
-    begin((ay[0], bx[0]))
-    gram(2, 5)
+        for copy in (ay, bx)[a][0]:
+            copy.start()
+    for half in range(2):
+        own = pl.ds(pl.multiple_of(half * HALF + place(half, 0) * LONG, 16), LONG)
+        total = gsend[own, :].astype(F32)
+        for k in around:
+            gram_out(half, k).wait_recv()
+            total = total + r1[half, k].astype(F32)
+        s1[half] = total
+        for k in around:
+            part_out(half, k).start()
     arrived((ay[2], bx[2]))
     begin((ay[1], bx[1]))
-    gram(5, 7)
     arrived((ay[3], bx[3]))
     begin((ax[0], by[0]))
-    gram(7, 10)
-
-    def piece(ref, k):
-        return ref.at[pl.ds(pl.multiple_of(k * PIECE, 16), PIECE), :]
-
-    def gram_out(k):
-        to = (ex + k) % N_EX
-        return remote(piece(gsend, to), grecv.at[k], g_s.at[k], g_r.at[k], {"ctx": ctx, "ex": to})
-
-    def sum_out(k):
-        to = (ex + k) % N_EX
-        return remote(piece(cb, ex), piece(cb, ex), c_s.at[k], c_r.at[k], {"ctx": ctx, "ex": to})
-
-    def sum_in(k):
-        of = (ex + N_EX - k) % N_EX
-        return remote(piece(cb, of), piece(cb, of), c_s.at[k], c_r.at[k], {"ctx": ctx, "ex": of})
-
-    def loop(body):
-        def step(k, carry):
-            body(k)
-            return carry
-
-        lax.fori_loop(1, N_EX, step, 0)
-
-    loop(lambda k: gram_out(k).start())
-    arrived((ax[2], by[2]))
-    begin((ax[1], by[1]))
-    def add_piece(k, total):
-        gram_out(k).wait_recv()
-        return total + grecv[k].astype(F32)
-
-    own_piece = gsend[pl.ds(pl.multiple_of(ex * PIECE, 16), PIECE), :].astype(F32)
-    total = lax.fori_loop(1, N_EX, add_piece, own_piece)
-    cb[pl.ds(pl.multiple_of(ex * PIECE, 16), PIECE), :] = total.astype(BF16)
-    loop(lambda k: sum_out(k).start())
+    for half in range(2):
+        total = s1[half, pl.ds(pl.multiple_of(place(half, 1) * SHORT, 16), SHORT), :]
+        for k in around:
+            part_out(half, k).wait_recv()
+            total = total + r2[half, k]
+        s2[half] = total
+        pair_out(half).start()
 
     load_x.wait()
     load_g.wait()
     for copy in swaps:
         copy.wait_recv()
+    rows = 2 * 128
+
+    def project(carry, xx, yy):
+        def step(n, carry):
+            xt, gt = carry
+            for l in range(2):
+                cols = pl.ds(pl.multiple_of(((n * 2 + l) * 4 + xx) * 256, 256), 256)
+                xt = xt + dot(xa[:, :, cols].reshape(rows, 256), wa[xx, n, l].reshape(128, 256), NT)
+                cols = pl.ds(pl.multiple_of(((yy * 2 + l) * 4 + n) * 256, 256), 256)
+                gt = gt + dot(wb[yy, n, l].reshape(128, 256), ga[:, :, cols].reshape(rows, 256), NT)
+            return xt, gt
+
+        return lax.fori_loop(0, 4, step, carry)
+
+    both = project((jnp.zeros((rows, 128), F32), jnp.zeros((128, rows), F32)), x, y)
+    for half in range(2):
+        pair_out(half).wait_recv()
+        own = pl.ds(pl.multiple_of(half * HALF + place(half, 0) * LONG + place(half, 1) * SHORT, 16), SHORT)
+        cb[own, :] = (s2[half] + r3[half]).astype(BF16)
+        for k in around:
+            spread_out(half, 1, k).start()
+    arrived((ax[2], by[2]))
+    begin((ax[1], by[1]))
+    both = project(both, xm, ym)
+    both = project(both, xp_, yp_)
     arrived((ax[3], by[3]))
-    rows = 2 * 128
-
-    def project(n, carry):
-        xt, gt = carry
-        yy, xx = n // 4, n % 4
-        for l in range(2):
-            e = (yy * 2 + l) * 4 + xx
-            cols = pl.ds(pl.multiple_of(e * 256, 256), 256)
-            xt = xt + dot(xa[:, :, cols].reshape(rows, 256), wa[xx, yy, l].reshape(128, 256), NT)
-            gt = gt + dot(wb[yy, xx, l].reshape(128, 256), ga[:, :, cols].reshape(rows, 256), NT)
-        return xt, gt
-
-    xt, gt = lax.fori_loop(0, 16, project, (jnp.zeros((rows, 128), F32), jnp.zeros((128, rows), F32)))
+    for half in range(2):
+        for k in around:
+            spread_out(half, 1, k, True).wait_recv()
+        for k in around:
+            spread_out(half, 0, k).start()
+    xt, gt = project(both, xo, yo)
     xt, gt = xt.astype(BF16), gt.astype(BF16)
     weights = jnp.concatenate([wm[0], wm[1]], axis=1)
     lane = lax.broadcasted_iota(jnp.int32, (32, 128), 1) // 32
@@ -271,9 +315,18 @@
         of = (ex + N_EX - k) % N_EX
         return remote(qs, queries_at(of), q_s.at[k], q_r.at[k], {"ctx": ctx, "ex": of})
 
+    def loop(body):
+        def step(k, carry):
+            body(k)
+            return carry
+
+        lax.fori_loop(1, N_EX, step, 0)
+
     loop(lambda k: q_out(k).start())
     qg[pl.ds(pl.multiple_of(ex * 32, 32), 32), :] = qs[...]
-    loop(lambda k: sum_in(k).wait_recv())
+    for half in range(2):
+        for k in around:
+            spread_out(half, 0, k, True).wait_recv()
     loop(lambda k: q_in(k).wait_recv())
 
     def curv(j, i):
@@ -332,14 +385,6 @@
         if n:
             hand_on(n - 1)
     hand_on(CHUNKS - 1)
-    score_scale = 1.0 / math.sqrt(MODULES * FEAT * LEN / DOCS)
-    for n in range(CHUNKS):
-        own = part[n, core, zh] + sib[n, zh]
-        for k in (1, 3, 2):
-            zo_out(n, k).wait_recv()
-            own = own + zrecv[n, k].astype(F32)
-        out[:, n * width : (n + 1) * width] = own * score_scale
-
     for d in range(1, 8):
         for a in range(2):
             along_z(d, a).wait_send()
@@ -348,27 +393,39 @@
     for four in (ay, bx, ax, by):
         for copy in four[0] + four[1]:
             copy.wait_send()
-    loop(lambda k: gram_out(k).wait_send())
-    loop(lambda k: sum_out(k).wait_send())
+    for half in range(2):
+        pair_out(half).wait_send()
+        for k in around:
+            gram_out(half, k).wait_send()
+            part_out(half, k).wait_send()
+            spread_out(half, 0, k).wait_send()
+            spread_out(half, 1, k).wait_send()
     loop(lambda k: q_out(k).wait_send())
     for k in (1, 2, 3):
         t_out(k).wait_send()
-        for n in range(CHUNKS):
-            zo_out(n, k).wait_send()
+    score_scale = 1.0 / math.sqrt(MODULES * FEAT * LEN / DOCS)
+    for n in range(CHUNKS):
+        own = part[n, core, zh] + sib[n, zh]
+        for k in (1, 3, 2):
+            zo_out(n, k).wait_recv()
+            own = own + zrecv[n, k].astype(F32)
+        out[:, n * width : (n + 1) * width] = own * score_scale
     for n in range(CHUNKS):
         o_out(n).wait_send()
+        for k in (1, 2, 3):
+            zo_out(n, k).wait_send()
 
 
 def shards(acts, out_grads, projections, segments, valid, stored):
     columns = jnp.transpose(projections, (0, 2, 1))
     vmem = pl.BlockSpec(memory_space=pltpu.VMEM)
-    hbm = pl.BlockSpec(memory_space=pl.ANY)
+    hbm = pl.BlockSpec(memory_space=pltpu.HBM)
     dma = pltpu.SemaphoreType.DMA
     width = 3072 // CHUNKS
     return pl.pallas_call(
         kernel,
         out_shape=jax.ShapeDtypeStruct((16, 3072), F32),
-        in_specs=[vmem, hbm, hbm, vmem, vmem, hbm],
+        in_specs=[hbm] * 6,
         out_specs=vmem,
         scratch_shapes=[
             pltpu.VMEM((4, 4, 2, 4, 32, 256), BF16),
@@ -376,10 +433,16 @@
             pltpu.VMEM((2, 128, 8192), BF16),
             pltpu.VMEM((2, 128, 8192), BF16),
             pltpu.VMEM((3072, FEAT), BF16),
+            pltpu.VMEM((1, 128), jnp.int32),
+            pltpu.VMEM((1, 128), jnp.int32),
             pltpu.VMEM((2, 8, 128), F32),
-            pltpu.VMEM((N_EX * PIECE, BLK), BF16),
-            pltpu.VMEM((N_EX, PIECE, BLK), BF16),
-            pltpu.VMEM((N_EX * PIECE, BLK), BF16),
+            pltpu.VMEM((2 * HALF, BLK), BF16),
+            pltpu.VMEM((2, 4, LONG, BLK), BF16),
+            pltpu.VMEM((2, LONG, BLK), F32),
+            pltpu.VMEM((2, 4, SHORT, BLK), F32),
+            pltpu.VMEM((2, SHORT, BLK), F32),
+            pltpu.VMEM((2, SHORT, BLK), F32),
+            pltpu.VMEM((2 * HALF, BLK), BF16),
             pltpu.VMEM((4, 32, 128), F32),
             pltpu.VMEM((4, 32, 128), F32),
             pltpu.VMEM((32, 128), F32),
@@ -388,17 +451,19 @@
             pltpu.VMEM((CHUNKS, 4, 16, width), F32),
             pltpu.VMEM((CHUNKS, 4, 16, width), BF16),
             pltpu.VMEM((CHUNKS, 4, 16, width), BF16),
-            dma((3,)),
+            dma((7,)),
             dma((3,)),
             dma((3,)),
             dma((2, 8)),
             dma((2, 8)),
             dma((16,)),
             dma((16,)),
-            dma((N_EX,)),
-            dma((N_EX,)),
-            dma((N_EX,)),
-            dma((N_EX,)),
+            dma((2, 2, 4)),
+            dma((2, 2, 4)),
+            dma((2,)),
+            dma((2,)),
+            dma((2, 2, 4)),
+            dma((2, 2, 4)),
             dma((4,)),
             dma((4,)),
             dma((N_EX,)),
@@ -409,7 +474,7 @@
             dma((CHUNKS, 4)),
         ],
         compiler_params=pltpu.CompilerParams(
-            collective_id=0, has_side_effects=True, vmem_limit_bytes=50 * 1024 * 1024
+            collective_id=0, has_side_effects=True, vmem_limit_bytes=60 * 1024 * 1024
         ),
         cost_estimate=pl.CostEstimate(flops=12_000_000_000, bytes_accessed=20_000_000, transcendentals=0),
     )(columns, acts, out_grads, segments, valid, stored)

time: 117 us -> 88.3 us (0.75)
  Pallas kernels: 113 us -> 86.1 us
  local copies, waits for them, and re-layouts: 4.34 us -> 1.62 us
    pallas_call x1, Pallas kernels: 113 us -> 86.1 us  [shards(): pl.pallas_call(kernel, out_shape=jax.ShapeDtypeStruct((16, 3072), F32), i...]
    unnamed x9 -> x1, local copies, waits for them, and re-layouts: 4.34 us -> 1.62 us
where the time goes in v2:
time: 88.3 us; the launch traced here: 87.8 us
  Pallas kernels  86.1 us (98%)
  local copies, waits for them, and re-layouts  1.62 us (2%)
    pallas_call x1, Pallas kernels, shards(): pl.pallas_call(kernel, out_shape=jax.ShapeDtypeStruct((16, 3072), F32), i...  86.1 us

profile of v2, /device:TPU:1, one launch (start us, length us, event | category | flops | bytes accessed | tf_op | source)
XLA Modules:
  0.0 87.8 jit_solution(6214642720257300721)
XLA Ops:
  0.0 86.1 %shard_map.64 = f32[16,3072]{1,0:T(8,128)} custom-call(bf16[2,32,256]{2,1,0:T(8,128)(2,1)} %bitcast.1, bf16[1,128,8192]{2,1,0:T(8,128)(2,1)} %acts.1, bf16[1,128,8192]{2,1,0:T(8,128)(2,1)} %grads.1, s32[1,128]{1,0:T(1,128)} %seg.1, s32[1,128]{1,0:T(1,128)} %val.1, bf16[3072,1024]{1,0:T(8,128)(2,1)} %stored.1), custom_call_target="tpu_custom_call" | custom-call | flops 12000000000 | bytes 20000000 | tf_op jit(solution)/shard_map/pallas_call | solution.py:425
  86.1 1.6 %copy.8 = f32[16,3072]{1,0:T(8,128)} copy(f32[16,3072]{1,0:T(8,128)} %shard_map.64) | data formatting | bytes 393216

commit v3 on v2

--- a/solution.py
+++ b/solution.py
@@ -24,7 +24,7 @@
 BF16 = jnp.bfloat16
 
 N_EX = 32
-CHUNKS = 4
+CHUNKS = 6
 BLK = 256
 NBLK = FEAT // BLK
 PAIRS = [(i, j) for i in range(NBLK) for j in range(i, NBLK)]
@@ -43,8 +43,8 @@
 
 def kernel(
     pt, acts, grads, seg, val, stored, out,
-    wa, wb, xa, ga, sv, sg, vl, wm, gsend, r1, s1, r2, s2, r3, cb, tsend, trecv, qs, qg, part, sib, zsend, zrecv,
-    loc_sem, sib_s, sib_r, z_s, z_r, ring_s, ring_r, rs_s, rs_r, zl_s, zl_r, ag_s, ag_r, t_s, t_r, q_s, q_r,
+    wa, wb, wca, wcb, xa, ga, sv, sg, vl, wm, gsend, r1, s1, s1b, r2, s2, s2b, r3, cb, tsend, trecv, qs, qsb, qg, qf, part, sib, zsend, zrecv,
+    loc_sem, sib_s, sib_r, z_s, z_r, ring_s, ring_r, cp_s, cp_r, cz_s, cz_r, rs_s, rs_r, zl_s, zl_r, ag_s, ag_r, t_s, t_r, q_s, q_r,
     o_s, o_r, zo_s, zo_r,
 ):
     ctx = lax.axis_index("ctx")
@@ -66,11 +66,13 @@
     load_s = pltpu.make_async_copy(stored, sv, loc_sem.at[0])
     load_x = pltpu.make_async_copy(acts.at[0], xa.at[0], loc_sem.at[1])
     load_g = pltpu.make_async_copy(grads.at[0], ga.at[0], loc_sem.at[2])
-    load_a = pltpu.make_async_copy(pt.at[0], wa.at[x, y, zl, zh], loc_sem.at[3])
-    load_b = pltpu.make_async_copy(pt.at[1], wb.at[y, x, zl, zh], loc_sem.at[4])
+    load_a = pltpu.make_async_copy(pt.at[0, :, 0:128], wa.at[x, y, zl, zh], loc_sem.at[3])
+    load_b = pltpu.make_async_copy(pt.at[1, :, 0:128], wb.at[y, x, zl, zh], loc_sem.at[4])
+    load_ca = pltpu.make_async_copy(pt.at[0, :, 128:256], wca.at[z, x, y], loc_sem.at[7])
+    load_cb = pltpu.make_async_copy(pt.at[1, :, 128:256], wcb.at[z, y, x], loc_sem.at[8])
     load_seg = pltpu.make_async_copy(seg, sg, loc_sem.at[5])
     load_val = pltpu.make_async_copy(val, vl, loc_sem.at[6])
-    for copy in (load_seg, load_val, load_a, load_b, load_s, load_x, load_g):
+    for copy in (load_seg, load_val, load_a, load_b, load_ca, load_cb, load_s, load_x, load_g):
         copy.start()
 
     barrier = pltpu.get_barrier_semaphore()
@@ -102,17 +104,48 @@
 
     def along_z(d, a):
         slot = wa.at[x, y, zl, zh] if a == 0 else wb.at[y, x, zl, zh]
-        return remote(pt.at[a], slot, z_s.at[a, d], z_r.at[a, d], at(x, y, (z + d) % 8))
+        return remote(pt.at[a, :, 0:128], slot, z_s.at[a, d], z_r.at[a, d], at(x, y, (z + d) % 8))
 
     def z_arrival(d, a):
         zz = (z + 8 - d) % 8
         slot = wa.at[x, y, zz % 2, zz // 2] if a == 0 else wb.at[y, x, zz % 2, zz // 2]
-        return remote(pt.at[a], slot, z_s.at[a, d], z_r.at[a, d], at(x, y, zz))
+        return remote(pt.at[a, :, 0:128], slot, z_s.at[a, d], z_r.at[a, d], at(x, y, zz))
+
+    def plane_out(a, stage, k, arriving=False):
+        along_x = (a == 1) == (stage == 0)
+        me = x if along_x else y
+        i = (me + 4 - k) % 4 if arriving else me
+        to = (me + k) % 4
+        if stage == 0:
+            block = wca.at[z, x, i] if a == 0 else wcb.at[z, y, i]
+            source = pt.at[a, :, 128:256]
+        else:
+            block = wca.at[z, i] if a == 0 else wcb.at[z, i]
+            source = block
+        return remote(
+            source, block, cp_s.at[a, stage, k], cp_r.at[a, stage, k], at(to, y, z) if along_x else at(x, to, z)
+        )
+
+    def round_z(t, arriving=False):
+        copies = []
+        for way in (0, 1):
+            sign = 1 if way == 0 else 7
+            for a in range(2):
+                if t == 4 and a != way:
+                    continue
+                zz = (z + (8 - sign) * (t if arriving else t - 1)) % 8
+                block = wca.at[zz] if a == 0 else wcb.at[zz]
+                copies.append(remote(block, block, cz_s.at[a, way, t], cz_r.at[a, way, t], at(x, y, (z + sign) % 8)))
+        return copies
 
     far = (4, 3, 5, 2, 6, 1, 7)
     for a in range(2):
         for d in far:
             along_z(d, a).start()
+    around = (2, 1, 3)
+    for k in around:
+        for a in range(2):
+            plane_out(a, 0, k).start()
     for copy in swaps:
         copy.start()
 
@@ -175,11 +208,11 @@
 
     def part_out(half, k):
         to = (place(half, 1) + k) % 4
-        source = rows_of(s1.at[half], to * SHORT, SHORT)
+        source = rows_of(s1b.at[half], to * SHORT, SHORT)
         return remote(source, r2.at[half, k], rs_s.at[half, 1, k], rs_r.at[half, 1, k], along(half, 1, to))
 
     def pair_out(half):
-        return remote(s2.at[half], r3.at[half], zl_s.at[half], zl_r.at[half], at(x, y, zh * 2 + 1 - zl))
+        return remote(s2b.at[half], r3.at[half], zl_s.at[half], zl_r.at[half], at(x, y, zh * 2 + 1 - zl))
 
     def short_block(half, j):
         return rows_of(cb, half * HALF + place(half, 0) * LONG + j * SHORT, SHORT)
@@ -193,12 +226,19 @@
         to = (me + k) % 4
         return remote(block, block, ag_s.at[half, stage, k], ag_r.at[half, stage, k], along(half, stage, to))
 
-    around = (2, 1, 3)
     load_s.wait()
     for half in range(2):
         gram(5 * half, 5 * half + 5)
         for k in around:
             gram_out(half, k).start()
+        if half == 0:
+            load_ca.wait()
+            load_cb.wait()
+            for a in range(2):
+                for k in around:
+                    plane_out(a, 0, k, True).wait_recv()
+                for k in around:
+                    plane_out(a, 1, k).start()
     load_a.wait()
     load_b.wait()
     for a in range(2):
@@ -206,6 +246,11 @@
             z_arrival(d, a).wait_recv()
         for copy in (ay, bx)[a][0]:
             copy.start()
+    for a in range(2):
+        for k in around:
+            plane_out(a, 1, k, True).wait_recv()
+    for copy in round_z(1):
+        copy.start()
     for half in range(2):
         own = pl.ds(pl.multiple_of(half * HALF + place(half, 0) * LONG, 16), LONG)
         total = gsend[own, :].astype(F32)
@@ -213,18 +258,28 @@
             gram_out(half, k).wait_recv()
             total = total + r1[half, k].astype(F32)
         s1[half] = total
+        s1b[half] = total.astype(BF16)
         for k in around:
             part_out(half, k).start()
+    def onward_z(t):
+        for copy in round_z(t, True):
+            copy.wait_recv()
+        if t < 4:
+            for copy in round_z(t + 1):
+                copy.start()
+
     arrived((ay[2], bx[2]))
     begin((ay[1], bx[1]))
     arrived((ay[3], bx[3]))
     begin((ax[0], by[0]))
+    onward_z(1)
     for half in range(2):
         total = s1[half, pl.ds(pl.multiple_of(place(half, 1) * SHORT, 16), SHORT), :]
         for k in around:
             part_out(half, k).wait_recv()
-            total = total + r2[half, k]
+            total = total + r2[half, k].astype(F32)
         s2[half] = total
+        s2b[half] = total.astype(BF16)
         pair_out(half).start()
 
     load_x.wait()
@@ -233,36 +288,64 @@
         copy.wait_recv()
     rows = 2 * 128
 
+    def lanes(ref, first, second):
+        return jnp.concatenate(
+            [ref[:, :, pl.ds(pl.multiple_of(c, 128), 128)].reshape(rows, 128) for c in (first, second)], axis=1
+        )
+
+    def beside(first, second):
+        return jnp.concatenate([first, second], axis=1)
+
     def project(carry, xx, yy):
         def step(n, carry):
             xt, gt = carry
-            for l in range(2):
-                cols = pl.ds(pl.multiple_of(((n * 2 + l) * 4 + xx) * 256, 256), 256)
-                xt = xt + dot(xa[:, :, cols].reshape(rows, 256), wa[xx, n, l].reshape(128, 256), NT)
-                cols = pl.ds(pl.multiple_of(((yy * 2 + l) * 4 + n) * 256, 256), 256)
-                gt = gt + dot(wb[yy, n, l].reshape(128, 256), ga[:, :, cols].reshape(rows, 256), NT)
+            c = (n * 8 + xx) * 256
+            block = beside(wa[xx, n, 0].reshape(128, 128), wa[xx, n, 1].reshape(128, 128))
+            xt = xt + dot(lanes(xa, c, c + 1024), block, NT)
+            c = (yy * 8 + n) * 256
+            block = beside(wb[yy, n, 0].reshape(128, 128), wb[yy, n, 1].reshape(128, 128))
+            gt = gt + dot(block, lanes(ga, c, c + 1024), NT)
             return xt, gt
 
         return lax.fori_loop(0, 4, step, carry)
 
+    def project_planes(carry, l):
+        def of(ref, i, j):
+            return jnp.concatenate([ref[2 * h + l, i, j] for h in range(4)], axis=0)
+
+        def step(n, carry):
+            xt, gt = carry
+            for p in range(2):
+                c = (n * 8 + l * 4 + 2 * p) * 256 + 128
+                xt = xt + dot(lanes(xa, c, c + 256), beside(of(wca, 2 * p, n), of(wca, 2 * p + 1, n)), NT)
+                gt = gt + dot(beside(of(wcb, n, 2 * p), of(wcb, n, 2 * p + 1)), lanes(ga, c, c + 256), NT)
+            return xt, gt
+
+        return lax.fori_loop(0, 4, step, carry)
+
     both = project((jnp.zeros((rows, 128), F32), jnp.zeros((128, rows), F32)), x, y)
+    onward_z(2)
     for half in range(2):
         pair_out(half).wait_recv()
         own = pl.ds(pl.multiple_of(half * HALF + place(half, 0) * LONG + place(half, 1) * SHORT, 16), SHORT)
-        cb[own, :] = (s2[half] + r3[half]).astype(BF16)
+        cb[own, :] = (s2[half] + r3[half].astype(F32)).astype(BF16)
         for k in around:
             spread_out(half, 1, k).start()
     arrived((ax[2], by[2]))
     begin((ax[1], by[1]))
     both = project(both, xm, ym)
     both = project(both, xp_, yp_)
+    onward_z(3)
+    both = project_planes(both, 1 - zl)
     arrived((ax[3], by[3]))
     for half in range(2):
         for k in around:
             spread_out(half, 1, k, True).wait_recv()
         for k in around:
             spread_out(half, 0, k).start()
-    xt, gt = project(both, xo, yo)
+    both = project(both, xo, yo)
+    onward_z(4)
+    xt, gt = project_planes(both, zl)
     xt, gt = xt.astype(BF16), gt.astype(BF16)
     weights = jnp.concatenate([wm[0], wm[1]], axis=1)
     lane = lax.broadcasted_iota(jnp.int32, (32, 128), 1) // 32
@@ -309,11 +392,11 @@
         return qg.at[pl.ds(pl.multiple_of(e * 32, 32), 32), :]
 
     def q_out(k):
-        return remote(qs, queries_at(ex), q_s.at[k], q_r.at[k], {"ctx": ctx, "ex": (ex + k) % N_EX})
+        return remote(qsb, queries_at(ex), q_s.at[k], q_r.at[k], {"ctx": ctx, "ex": (ex + k) % N_EX})
 
     def q_in(k):
         of = (ex + N_EX - k) % N_EX
-        return remote(qs, queries_at(of), q_s.at[k], q_r.at[k], {"ctx": ctx, "ex": of})
+        return remote(qsb, queries_at(of), q_s.at[k], q_r.at[k], {"ctx": ctx, "ex": of})
 
     def loop(body):
         def step(k, carry):
@@ -322,12 +405,14 @@
 
         lax.fori_loop(1, N_EX, step, 0)
 
+    qsb[...] = qs[...].astype(BF16)
     loop(lambda k: q_out(k).start())
-    qg[pl.ds(pl.multiple_of(ex * 32, 32), 32), :] = qs[...]
+    qg[pl.ds(pl.multiple_of(ex * 32, 32), 32), :] = qsb[...]
     for half in range(2):
         for k in around:
             spread_out(half, 0, k, True).wait_recv()
     loop(lambda k: q_in(k).wait_recv())
+    qf[...] = qg[...].astype(F32)
 
     def curv(j, i):
         n = PAIRS.index((min(i, j), max(i, j)))
@@ -342,7 +427,7 @@
     step_size = 1.0 / (spread * (mean_diag + epsilon))
 
     queries = [
-        jnp.concatenate([qg[pl.ds(2 * i + h, 128, stride=8), :] for h in range(2)], axis=1) for i in range(NBLK)
+        jnp.concatenate([qf[pl.ds(2 * i + h, 128, stride=8), :] for h in range(2)], axis=1) for i in range(NBLK)
     ]
     iterate = [step_size * q for q in queries]
     for _ in range(STEPS):
@@ -390,6 +475,13 @@
             along_z(d, a).wait_send()
     for copy in swaps:
         copy.wait_send()
+    for t in range(1, 5):
+        for copy in round_z(t):
+            copy.wait_send()
+    for a in range(2):
+        for k in around:
+            plane_out(a, 0, k).wait_send()
+            plane_out(a, 1, k).wait_send()
     for four in (ay, bx, ax, by):
         for copy in four[0] + four[1]:
             copy.wait_send()
@@ -428,8 +520,10 @@
         in_specs=[hbm] * 6,
         out_specs=vmem,
         scratch_shapes=[
-            pltpu.VMEM((4, 4, 2, 4, 32, 256), BF16),
-            pltpu.VMEM((4, 4, 2, 4, 32, 256), BF16),
+            pltpu.VMEM((4, 4, 2, 4, 32, 128), BF16),
+            pltpu.VMEM((4, 4, 2, 4, 32, 128), BF16),
+            pltpu.VMEM((8, 4, 4, 32, 128), BF16),
+            pltpu.VMEM((8, 4, 4, 32, 128), BF16),
             pltpu.VMEM((2, 128, 8192), BF16),
             pltpu.VMEM((2, 128, 8192), BF16),
             pltpu.VMEM((3072, FEAT), BF16),
@@ -439,25 +533,33 @@
             pltpu.VMEM((2 * HALF, BLK), BF16),
             pltpu.VMEM((2, 4, LONG, BLK), BF16),
             pltpu.VMEM((2, LONG, BLK), F32),
-            pltpu.VMEM((2, 4, SHORT, BLK), F32),
+            pltpu.VMEM((2, LONG, BLK), BF16),
+            pltpu.VMEM((2, 4, SHORT, BLK), BF16),
             pltpu.VMEM((2, SHORT, BLK), F32),
-            pltpu.VMEM((2, SHORT, BLK), F32),
+            pltpu.VMEM((2, SHORT, BLK), BF16),
+            pltpu.VMEM((2, SHORT, BLK), BF16),
             pltpu.VMEM((2 * HALF, BLK), BF16),
             pltpu.VMEM((4, 32, 128), F32),
             pltpu.VMEM((4, 32, 128), F32),
             pltpu.VMEM((32, 128), F32),
+            pltpu.VMEM((32, 128), BF16),
+            pltpu.VMEM((N_EX * 32, 128), BF16),
             pltpu.VMEM((N_EX * 32, 128), F32),
             pltpu.VMEM((CHUNKS, 2, 4, 16, width), F32),
             pltpu.VMEM((CHUNKS, 4, 16, width), F32),
             pltpu.VMEM((CHUNKS, 4, 16, width), BF16),
             pltpu.VMEM((CHUNKS, 4, 16, width), BF16),
-            dma((7,)),
+            dma((9,)),
             dma((3,)),
             dma((3,)),
             dma((2, 8)),
             dma((2, 8)),
             dma((16,)),
             dma((16,)),
+            dma((2, 2, 4)),
+            dma((2, 2, 4)),
+            dma((2, 2, 5)),
+            dma((2, 2, 5)),
             dma((2, 2, 4)),
             dma((2, 2, 4)),
             dma((2,)),

time: 88.3 us -> 83.6 us (0.947)
  Pallas kernels: 86.1 us -> 81.2 us
    pallas_call x1, Pallas kernels: 86.1 us -> 81.2 us  [shards(): pl.pallas_call(kernel, out_shape=jax.ShapeDtypeStruct((16, 3072), F32), i...]
where the time goes in v3:
time: 83.6 us; the launch traced here: 82.8 us
  Pallas kernels  81.2 us (97%)
  local copies, waits for them, and re-layouts  1.62 us (2%)
    pallas_call x1, Pallas kernels, shards(): pl.pallas_call(kernel, out_shape=jax.ShapeDtypeStruct((16, 3072), F32), i...  81.2 us

profile of v3, /device:TPU:1, one launch (start us, length us, event | category | flops | bytes accessed | tf_op | source)
XLA Modules:
  0.0 82.8 jit_solution(4685496247780839767)
XLA Ops:
  0.0 81.2 %shard_map.64 = f32[16,3072]{1,0:T(8,128)} custom-call(bf16[2,32,256]{2,1,0:T(8,128)(2,1)} %bitcast.1, bf16[1,128,8192]{2,1,0:T(8,128)(2,1)} %acts.1, bf16[1,128,8192]{2,1,0:T(8,128)(2,1)} %grads.1, s32[1,128]{1,0:T(1,128)} %seg.1, s32[1,128]{1,0:T(1,128)} %val.1, bf16[3072,1024]{1,0:T(8,128)(2,1)} %stored.1), custom_call_target="tpu_custom_call" | custom-call | flops 12000000000 | bytes 20000000 | tf_op jit(solution)/shard_map/pallas_call | solution.py:517
  81.2 1.6 %copy.8 = f32[16,3072]{1,0:T(8,128)} copy(f32[16,3072]{1,0:T(8,128)} %shard_map.64) | data formatting | bytes 393216

commit v4 on v3

--- a/solution.py
+++ b/solution.py
@@ -24,7 +24,7 @@
 BF16 = jnp.bfloat16
 
 N_EX = 32
-CHUNKS = 6
+CHUNKS = 8
 BLK = 256
 NBLK = FEAT // BLK
 PAIRS = [(i, j) for i in range(NBLK) for j in range(i, NBLK)]
@@ -128,9 +128,9 @@
 
     def round_z(t, arriving=False):
         copies = []
-        for way in (0, 1):
-            sign = 1 if way == 0 else 7
-            for a in range(2):
+        for a in range(2):
+            for way in (0, 1):
+                sign = 1 if way == 0 else 7
                 if t == 4 and a != way:
                     continue
                 zz = (z + (8 - sign) * (t if arriving else t - 1)) % 8
@@ -262,10 +262,11 @@
         for k in around:
             part_out(half, k).start()
     def onward_z(t):
-        for copy in round_z(t, True):
-            copy.wait_recv()
-        if t < 4:
-            for copy in round_z(t + 1):
+        coming, going = round_z(t, True), round_z(t + 1) if t < 4 else []
+        for a in range(2):
+            for copy in coming[a * len(coming) // 2 : (a + 1) * len(coming) // 2]:
+                copy.wait_recv()
+            for copy in going[a * len(going) // 2 : (a + 1) * len(going) // 2]:
                 copy.start()
 
     arrived((ay[2], bx[2]))

time: 83.6 us -> 83.5 us (level)
  no operation moved by 1% of the time
where the time goes in v4:
time: 83.5 us; the launch traced here: 83.2 us
  Pallas kernels  81.5 us (98%)
  local copies, waits for them, and re-layouts  1.62 us (2%)
    pallas_call x1, Pallas kernels, shards(): pl.pallas_call(kernel, out_shape=jax.ShapeDtypeStruct((16, 3072), F32), i...  81.5 us

profile of v4, /device:TPU:1, one launch (start us, length us, event | category | flops | bytes accessed | tf_op | source)
XLA Modules:
  0.0 83.2 jit_solution(7153870213424370226)
XLA Ops:
  0.0 81.5 %shard_map.64 = f32[16,3072]{1,0:T(8,128)} custom-call(bf16[2,32,256]{2,1,0:T(8,128)(2,1)} %bitcast.1, bf16[1,128,8192]{2,1,0:T(8,128)(2,1)} %acts.1, bf16[1,128,8192]{2,1,0:T(8,128)(2,1)} %grads.1, s32[1,128]{1,0:T(1,128)} %seg.1, s32[1,128]{1,0:T(1,128)} %val.1, bf16[3072,1024]{1,0:T(8,128)(2,1)} %stored.1), custom_call_target="tpu_custom_call" | custom-call | flops 12000000000 | bytes 20000000 | tf_op jit(solution)/shard_map/pallas_call | solution.py:518
  81.5 1.6 %copy.8 = f32[16,3072]{1,0:T(8,128)} copy(f32[16,3072]{1,0:T(8,128)} %shard_map.64) | data formatting | bytes 393216
